TPU v7x, 512 devices: a whole 4x4x16 slice. The times are simulated.
512 devices in a mesh: dp: 32 (over x, y, core), seq: 16 (over z).
Axes of the slice: x: 4, y: 4, z: 16, core: 2. Of those that a mesh axis runs over, the one named last changes fastest.
Arguments:
- tile_tokens: bfloat16 [32, 512, 3200], P('dp', 'seq'), may hold values from -6 to 6
- proj_weight: bfloat16 [3200, 8192], P('dp', 'seq')
- text_hidden: bfloat16 [32, 2048, 8192], P('dp', 'seq'), may hold values from -6 to 6
- cotangent: bfloat16 [32, 2048, 8192], P('dp', 'seq'), may hold values from -1.1953125 to 1.1953125
- norm_gain: float32 [8192], replicated, may hold values from 0.25 to 1.75
- placeholders: int32 [32, 512], P('dp'), may hold values from 0 to 2047, as said below
- bucket_levels: int32 [32, 16, 3200], P('dp', 'seq'), may hold values from 2 to 16
- row_draws: float32 [32, 16, 3200], P('dp', 'seq'), may hold values from 0 to 1
- column_draws: float32 [32, 8192], P('dp', 'seq'), may hold values from 0 to 1
Outputs:
- weight_grad: float32 [3200, 8192], P('dp', 'seq')
- gain_grad: float32 [8192], replicated
Inputs may be any that keep to these rules, and one draw needn't show every extreme that they name: Each row is strictly increasing. Among the positions of one device's block of 128 positions stand at most 48 placeholders, and in every row some block holds exactly 48.
All inputs are finite; a program needn't handle non-finite values.
Results may differ from a plain program's by a relative error of at most 0.014.
Values may be sent and summed in bfloat16 or wider, within the bound.
A program may use at most 64 MiB of HBM per device.

v0:
```python
import jax
import jax.numpy as jnp
from jax import lax
from jax.sharding import Mesh
from jax.sharding import PartitionSpec as P

IMG_MOST = 48
DP = ("dp_0", "dp_1", "dp_2")
DP_SEQ = ("dp_0", "dp_1", "dp_2", "seq")
EPSILON = 1e-06


def copy_for_each(value, axis):
    copies = jnp.broadcast_to(value, (lax.axis_size(axis), *value.shape))
    return lax.all_to_all(copies, axis, split_axis=0, concat_axis=0, tiled=True)


def of_everyone(value, axis):
    everything = copy_for_each(value, axis)
    return jnp.sum(everything, axis=0)


def in_one(arrays, axis):
    ravelled, at, outs = (jnp.concatenate([a.reshape(-1) for a in arrays]), 0, [])
    so_far = of_everyone(ravelled, axis)
    for a in arrays:
        outs.append(so_far[at : at + a.size].reshape(a.shape))
        at += a.size
    return tuple(outs)


def one_axis_at_a_time(value, axes):
    for axis in axes:
        value = lax.psum(value, axis)
    return value


def quantize(gradient, levels_now, rows_now, columns_now):
    bucket_norm = jnp.sqrt(jnp.sum(gradient * gradient, axis=1, keepdims=True) + EPSILON)
    step_count = levels_now.astype(jnp.float32)[:, None]
    offset = 0.25 + 0.25 * (rows_now[:, None] + columns_now[None, :])
    ratio = jnp.abs(gradient) / bucket_norm * step_count
    lower = jnp.floor(ratio)
    quantum = lower + jnp.clip(2.0 * (ratio - lower - offset) + 0.5, 0.0, 1.0)
    return jnp.sign(gradient) * bucket_norm * quantum / step_count


def on_device(
    tile_tokens,
    proj_weight,
    text_hidden,
    cotangent,
    norm_gain,
    placeholders,
    bucket_levels,
    row_draws,
    column_draws,
):
    seq_count = lax.axis_size("seq")
    seq_index = lax.axis_index("seq")
    replicas = lax.axis_size(DP)
    places = placeholders[0]
    image_total = places.shape[0]
    tok_rows = text_hidden.shape[1]
    model_width = text_hidden.shape[2]
    columns = proj_weight.shape[1]
    all_positions = tok_rows * seq_count
    zero_half = jnp.zeros((), jnp.bfloat16)
    own_text = text_hidden[0]
    own_cot = cotangent[0]
    gathered = lax.all_gather(tile_tokens[0], "seq", axis=0, tiled=True)
    patch_block = gathered
    embedded = jnp.dot(
        patch_block,
        lax.all_gather(proj_weight, DP, axis=0, tiled=True),
        preferred_element_type=jnp.float32,
    ).astype(jnp.bfloat16)
    image_marks = jnp.zeros((all_positions,), jnp.int32).at[places].set(1)
    local_marks = lax.dynamic_slice_in_dim(image_marks, seq_index * tok_rows, tok_rows)
    is_image = local_marks[:, None] == 1
    owners = places // tok_rows
    owner_ids = jnp.arange(seq_count, dtype=jnp.int32)
    counts = jnp.sum((owners[:, None] == owner_ids[None, :]).astype(jnp.int32), axis=0)
    starts = jnp.cumsum(counts) - counts
    own_start = starts[seq_index]
    own_count = counts[seq_index]
    slot_ids = jnp.arange(IMG_MOST, dtype=jnp.int32)
    source_rows = jnp.clip(own_start + slot_ids, 0, image_total - 1)
    local_slots = jnp.clip(jnp.take(places, source_rows) - seq_index * tok_rows, 0, tok_rows - 1)
    slot_live = (slot_ids < own_count)[:, None]
    flat_index = owners * IMG_MOST + (
        jnp.arange(image_total, dtype=jnp.int32) - jnp.take(starts, owners)
    )
    outgoing = jnp.where(slot_live, jnp.take(own_cot, local_slots, axis=0), zero_half)
    returned = lax.all_to_all(outgoing[None], "seq", split_axis=2, concat_axis=0, tiled=True)
    image_cot = jnp.take(returned.reshape(-1, columns), flat_index, axis=0).astype(jnp.float32)
    emb_float = embedded.astype(jnp.float32)
    column_gain = lax.dynamic_slice_in_dim(norm_gain, seq_index * columns, columns)
    grad_in = image_cot * column_gain[None, :]
    squares, mixed = in_one(
        (jnp.sum(emb_float * emb_float, axis=1), jnp.sum(grad_in * emb_float, axis=1)), "seq"
    )
    inverse = lax.rsqrt(squares / model_width + EPSILON)[:, None]
    normed = emb_float * inverse
    emb_grad = ((grad_in - normed * (mixed[:, None] * inverse / model_width)) * inverse).astype(
        jnp.bfloat16
    )
    image_part = jnp.sum(image_cot * normed, axis=0)
    text_float = own_text.astype(jnp.float32)
    text_inverse = lax.rsqrt(jnp.mean(text_float * text_float, axis=1, keepdims=True) + EPSILON)
    text_terms = own_cot.astype(jnp.float32) * text_float * text_inverse
    text_part = jnp.sum(jnp.where(is_image, 0.0, text_terms), axis=0)
    placed_part = lax.dynamic_update_slice_in_dim(
        jnp.zeros((model_width,), jnp.float32), image_part, seq_index * columns, 0
    )
    gain_part = text_part + placed_part
    own_levels = bucket_levels[0, 0]
    own_row_draws = row_draws[0, 0]
    own_column_draws = column_draws[0]
    patch_block = gathered
    gradient = lax.dot_general(
        patch_block, emb_grad, (((0,), (0,)), ((), ())), preferred_element_type=jnp.float32
    )
    summed = lax.psum_scatter(
        quantize(gradient, own_levels, own_row_draws, own_column_draws).astype(jnp.bfloat16),
        DP,
        scatter_dimension=0,
        tiled=True,
    ).astype(jnp.float32)
    gain_total = one_axis_at_a_time(gain_part, DP_SEQ)
    return (summed / replicas, gain_total / replicas)


def solution(mesh):
    finer = Mesh(mesh.devices.reshape(4, 4, 2, mesh.shape["seq"]), ("dp_0", "dp_1", "dp_2", "seq"))
    return jax.shard_map(
        on_device,
        mesh=finer,
        in_specs=(
            P(DP, "seq", None),
            P(DP, "seq"),
            P(DP, "seq", None),
            P(DP, "seq", None),
            P(),
            P(DP, None),
            P(DP, "seq", None),
            P(DP, "seq", None),
            P(DP, "seq"),
        ),
        out_specs=(P(DP, "seq"), P()),
        check_vma=False,
    )
```

profile of v0, /device:TPU:6, one launch (start us, length us, event | category | flops | bytes accessed | tf_op | source)
XLA Modules:
  0.0 358.7 jit_solution(13340607720197606231)
XLA Ops:
  7.2 0.7 all-gather.7.cloned.1.call-update
  7.9 0.7 all-gather.5.cloned.1.call-update
  8.6 0.7 add_select_fusion
  9.7 0.6 dynamic_slice.12
  10.3 0.7 fusion.39
  11.1 0.7 fusion.37
  11.8 1.5 gather_fusion
  13.2 0.7 fusion.36
  13.9 3.6 %gather_fusion.1 = bf16[48,8192]{1,0:T(8,128)(2,1)S(1)} fusion(bf16[128,8192]{1,0:T(8,128)(2,1)} %bitcast.91, s32[1024]{0:T(1024)S(1)} %pad_clamp_fusion.1), kind=kCustom, calls=%fused_computation.1 | custom fusion | bytes 1573056 | tf_op jit(solution)/shard_map/jit(_take)/gather | solution.py:94
  17.6 1.3 compare_and_fusion
  18.9 0.2 fusion.25
  19.0 6.8 %copy.37 = bf16[1,48,8192]{1,0,2:T(2,128)(2,1)} copy(bf16[1,48,8192]{2,1,0:T(8,128)(2,1)S(1)} %fusion.25) | data formatting | bytes 1572864 | tf_op jit(solution)/shard_map/jit(_where)/select_n | solution.py:94
  25.9 0.5 broadcast.663
  26.4 45.1 %reduce.24 = bf16[8192,48]{1,0:T(8,128)(2,1)S(1)} reduce(bf16[8192,1,48]{2,1,0:T(2,128)(2,1)} %bitcast.93, bf16[]{:T(256)} %broadcast.663), dimensions={1}, to_apply=%bitcast.79.reduce_sub_computation | reduce | bytes 1572866
  71.5 3.9 %reshape.481 = bf16[16,2,12288]{2,1,0:T(2,128)(2,1)} reshape(bf16[8192,48]{1,0:T(8,128)(2,1)S(1)} %reduce.24) | data formatting | bytes 1572864
  75.4 15.2 %all-to-all-start = ((bf16[16,2,12288]{2,1,0:T(2,128)(2,1)}), bf16[16,2,12288]{2,1,0:T(2,128)(2,1)S(1)}, u32[]{:S(2)}, u32[]{:S(2)}) async-start(bf16[16,2,12288]{2,1,0:T(2,128)(2,1)} %reshape.481), calls=%async_computation | async-start | bytes 1572864 | tf_op jit(solution)/shard_map/all_to_all | solution.py:95
  90.6 0.8 dynamic_slice.14
  91.4 4.3 %compare_select_fusion.2 = (s32[512,1]{0,1:T(1,128)S(1)}, s32[512,1]{0,1:T(1,128)S(1)}, s32[512,1]{0,1:T(1,128)S(1)}, s32[512,1]{0,1:T(1,128)S(1)}) fusion(s32[]{:T(128)} %bitcast.12, s32[]{:T(128)} %bitcast.13, s32[]{:T(128)} %bitcast.14, s32[]{:T(128)} %bitcast.15, s32[]{:T(128)} %bitcast.16, s32[]{:T(128)} %bitcast.18, s32[]{:T(128)} %bitcast.17, ...), kind=kLoop, calls=%fused_computation.62 | loop fusion | flops 16384 | bytes 10268 | tf_op jit(solution)/shard_map/jit(_take)/gather | solution.py:92
  95.8 5.8 %compare_and_fusion.1 = (pred[512]{0:T(512)(128)(4,1)S(1)}, s32[512]{0:T(512)S(1)}) fusion(pred[512]{0:T(512)(128)(4,1)S(1)} %get-tuple-element.24, pred[512]{0:T(512)(128)(4,1)S(1)} %get-tuple-element.22, pred[512]{0:T(512)(128)(4,1)S(1)} %get-tuple-element.23, pred[512]{0:T(512)(128)(4,1)S(1)} %get-tuple-element.21, ...), kind=kLoop, calls=%fused_computation.102 | loop fusion | flops 20480 | bytes 11300 | tf_op jit(solution)/shard_map/jit(_take)/and | solution.py:96
  101.6 36.3 %all-to-all-done = bf16[16,2,12288]{2,1,0:T(2,128)(2,1)S(1)} async-done(((bf16[16,2,12288]{2,1,0:T(2,128)(2,1)}), bf16[16,2,12288]{2,1,0:T(2,128)(2,1)S(1)}, u32[]{:S(2)}, u32[]{:S(2)}) %all-to-all-start) | async-done | bytes 786464 | tf_op jit(solution)/shard_map/all_to_all | solution.py:95
  137.9 7.9 %reshape.482 = bf16[8192,1,48]{2,1,0:T(2,128)(2,1)} reshape(bf16[16,2,12288]{2,1,0:T(2,128)(2,1)S(1)} %all-to-all-done) | data formatting | bytes 1572864
  145.8 8.1 %copy.38 = bf16[1,48,8192]{2,1,0:T(8,128)(2,1)S(1)} copy(bf16[1,48,8192]{1,0,2:T(2,128)(2,1)} %bitcast.94) | data formatting | bytes 1572864 | tf_op jit(solution)/shard_map/all_to_all | solution.py:95
  154.0 0.2 copy.48
  154.3 0.4 copy.39
  154.7 2.0 gather_fusion.2
  156.7 1.0 copy.40
  157.7 3.7 %reshape.455 = bf16[3200,512]{1,0:T(8,128)(2,1)S(1)} reshape(bf16[32,100,512]{2,1,0:T(8,128)(2,1)} %all-gather.7.cloned.1.call-done) | data formatting | bytes 6553600
  161.5 19.4 %all-gather.5.cloned.1.call-done = bf16[1,512,3200]{2,1,0:T(8,128)(2,1)} async-done(((bf16[1,32,3200]{2,1,0:T(8,128)(2,1)}), bf16[1,512,3200]{2,1,0:T(8,128)(2,1)}) %all-gather.5.cloned.1.call-update) | async-done | bytes 3276816 | tf_op jit(solution)/shard_map/all_gather | solution.py:71
  180.8 4.9 %fusion.23 = (f32[512]{0:T(512)S(1)}, f32[512]{0:T(512)S(1)}, bf16[512,512]{0,1:T(8,128)(2,1)}) fusion(f32[512]{0:T(512)S(1)} %dynamic_slice.14, bf16[512,512]{0,1:T(8,128)(2,1)} %copy.40, pred[512]{0:T(512)(128)(4,1)S(1)} %get-tuple-element.25, bf16[3200,512]{1,0:T(8,128)(2,1)S(1)} %reshape.455, bf16[1,512,3200]{2,1,0:T(8,128)(2,1)} %all-gather.5.cloned.1.call-done), kind=kOutput, calls=%fused_computation.35 | convolution fusion | flops 1680079872 | bytes 7608832 | tf_op jit(solution)/shard_map/dot_general | solution.py:73
  185.7 0.7 broadcast_in_dim.90
  186.4 6.6 %all-to-all-start.1 = ((f32[16,1,1024]{2,1,0:T(1,128)}), f32[16,1,1024]{2,1,0:T(1,128)S(1)}, u32[]{:S(2)}, u32[]{:S(2)}) async-start(f32[16,1,1024]{2,1,0:T(1,128)} %broadcast_in_dim.90), calls=%async_computation.1 | async-start | bytes 131072 | tf_op jit(solution)/shard_map/all_to_all | solution.py:15
  193.1 2.7 scatter_custom_fusion
  195.8 10.0 %all-to-all-done.1 = f32[16,1,1024]{2,1,0:T(1,128)S(1)} async-done(((f32[16,1,1024]{2,1,0:T(1,128)}), f32[16,1,1024]{2,1,0:T(1,128)S(1)}, u32[]{:S(2)}, u32[]{:S(2)}) %all-to-all-start.1) | async-done | bytes 65568 | tf_op jit(solution)/shard_map/all_to_all | solution.py:15
  205.9 4.4 %multiply_reduce_fusion = (f32[3200]{0:T(1024)S(1)}, f32[512,3200]{1,0:T(8,128)S(1)}) fusion(bf16[1,512,3200]{2,1,0:T(8,128)(2,1)} %all-gather.5.cloned.1.call-done, bf16[512,512]{0,1:T(8,128)(2,1)} %get-tuple-element.50, f32[512]{0:T(512)S(1)} %get-tuple-element.31, f32[512]{0:T(512)S(1)} %get-tuple-element.30, f32[512]{0:T(512)S(1)} %dynamic_slice.14, ...), kind=kOutput, calls=%fused_computation.12 | convolution fusion | flops 1683354496 | bytes 10898432 | tf_op jit(solution)/shard_map/dot_general | solution.py:121
  210.3 6.5 %fusion.6 = bf16[3200,512]{0,1:T(8,128)(2,1)} fusion(f32[512,3200]{1,0:T(8,128)S(1)} %get-tuple-element.52, f32[3200]{0:T(1024)S(1)} %convert_reduce_fusion.1, f32[512]{0:T(512)S(1)} %bitcast.103, f32[3200]{0:T(1024)S(1)} %reduce.13, f32[3200]{0:T(1024)S(1)} %add_sqrt_fusion), kind=kLoop, calls=%fused_computation.13 | loop fusion | flops 29491200 | bytes 9870848 | tf_op jit(solution)/shard_map/convert_element_type | solution.py:125
  216.9 1.4 dynamic-slice.1
  218.9 2.1 fusion.10
  221.0 2.5 fusion.9
  223.5 0.3 fusion.22
  223.8 0.2 add_dynamic-update-slice_fusion
  224.0 14.2 %psum.28 = f32[8192]{0:T(1024)S(1)} all-reduce(f32[8192]{0:T(1024)S(1)} %add_dynamic-update-slice_fusion), channel_id=1, replica_groups=mesh['dp_0'=4,'dp_1'=4,'dp_2'=2,'seq'=16] {'dp_0'}, use_global_device_ids=true, to_apply=%region_11.12 | all-reduce | flops 8192 | bytes 65536 | tf_op jit(solution)/shard_map/psum | solution.py:34
  238.2 17.1 %psum.29 = f32[8192]{0:T(1024)S(1)} all-reduce(f32[8192]{0:T(1024)S(1)} %psum.28), channel_id=1, replica_groups=mesh['dp_0'=4,'dp_1'=4,'dp_2'=2,'seq'=16] {'dp_1'}, use_global_device_ids=true, to_apply=%region_12.13 | all-reduce | flops 8192 | bytes 65536 | tf_op jit(solution)/shard_map/psum | solution.py:34
  255.3 3.4 psum.30
  258.7 54.0 %psum.31 = f32[8192]{0:T(1024)S(1)} all-reduce(f32[8192]{0:T(1024)S(1)} %psum.30), channel_id=1, replica_groups=mesh['dp_0'=4,'dp_1'=4,'dp_2'=2,'seq'=16] {'seq'}, use_global_device_ids=true, to_apply=%region_14.15 | all-reduce | flops 8192 | bytes 65536 | tf_op jit(solution)/shard_map/psum | solution.py:34
  312.7 0.6 broadcast_multiply_fusion
  313.3 37.0 %all-reduce.3.cloned.1.call-done = bf16[3200,512]{0,1:T(8,128)(2,1)} async-done(((bf16[3200,512]{0,1:T(8,128)(2,1)}), bf16[3200,512]{0,1:T(8,128)(2,1)}) %all-reduce.3.cloned.1.call-update) | async-done | bytes 3276816
  350.3 1.1 convert_multiply_fusion.7
  351.4 0.8 copy.42
  (39 shorter events, 0.9 us)
Async XLA Ops:
  7.2 150.5 %all-gather.7.cloned.1.call-start = ((), (), s32[]{:S(2)}) async-start(), calls=%async_computation.3 | async-start | bytes 3514368 | tf_op jit(solution)/shard_map/all_gather | solution.py:75
  7.9 172.9 %all-gather.5.cloned.1.call-start = ((), (), s32[]{:S(2)}) async-start(), calls=%async_computation.2 | async-start | bytes 3481600 | tf_op jit(solution)/shard_map/all_gather | solution.py:71
  26.4 65.0 %copy-start = (s32[1,512]{1,0:T(1,128)S(1)}, s32[1,512]{1,0:T(1,128)}, u32[]{:S(2)}) copy-start(s32[1,512]{1,0:T(1,128)} %param.14) | copy-start | bytes 6148
  75.4 62.5 %all-to-all-start = ((bf16[16,2,12288]{2,1,0:T(2,128)(2,1)}), bf16[16,2,12288]{2,1,0:T(2,128)(2,1)S(1)}, u32[]{:S(2)}, u32[]{:S(2)}) async-start(bf16[16,2,12288]{2,1,0:T(2,128)(2,1)} %reshape.481), calls=%async_computation | async-start | bytes 1572864 | tf_op jit(solution)/shard_map/all_to_all | solution.py:95
  180.8 12.2 %copy-start.5 = (f32[1,1,3200]{2,1,0:T(1,128)S(1)}, f32[1,1,3200]{2,1,0:T(1,128)}, u32[]{:S(2)}) copy-start(f32[1,1,3200]{2,1,0:T(1,128)} %param.16) | copy-start | bytes 38404
  180.8 14.9 %copy-start.4 = (s32[1,1,3200]{2,1,0:T(1,128)S(1)}, s32[1,1,3200]{2,1,0:T(1,128)}, u32[]{:S(2)}) copy-start(s32[1,1,3200]{2,1,0:T(1,128)} %param.15) | copy-start | bytes 38404
  186.4 19.4 %all-to-all-start.1 = ((f32[16,1,1024]{2,1,0:T(1,128)}), f32[16,1,1024]{2,1,0:T(1,128)S(1)}, u32[]{:S(2)}, u32[]{:S(2)}) async-start(f32[16,1,1024]{2,1,0:T(1,128)} %broadcast_in_dim.90), calls=%async_computation.1 | async-start | bytes 131072 | tf_op jit(solution)/shard_map/all_to_all | solution.py:15
  193.0 157.3 %all-reduce.3.cloned.1.call-start = ((), (), s32[]{:S(2)}) async-start(), calls=%async_computation.4 | async-start | bytes 6553600
  205.9 4.4 %copy-start.6 = (f32[1,512]{1,0:T(1,128)S(1)}, f32[1,512]{1,0:T(1,128)}, u32[]{:S(2)}) copy-start(f32[1,512]{1,0:T(1,128)} %param.17) | copy-start | bytes 6148
  216.8 4.3 %copy-start.1 = (bf16[1,128,8192]{2,1,0:T(8,128)(2,1)S(1)}, bf16[1,128,8192]{2,1,0:T(8,128)(2,1)}, u32[]{:S(2)}) copy-start(bf16[1,128,8192]{2,1,0:T(8,128)(2,1)} %param.12) | copy-start | bytes 6291460
  216.8 6.8 %copy-start.2 = (bf16[512,512]{0,1:T(8,128)(2,1)S(1)}, bf16[512,512]{0,1:T(8,128)(2,1)}, u32[]{:S(2)}) copy-start(bf16[512,512]{0,1:T(8,128)(2,1)} %copy.40) | copy-start | bytes 1572868
  216.8 6.8 %copy-start.3 = (bf16[512,512]{0,1:T(8,128)(2,1)S(1)}, bf16[512,512]{0,1:T(8,128)(2,1)}, u32[]{:S(2)}) copy-start(bf16[512,512]{0,1:T(8,128)(2,1)} %get-tuple-element.50) | copy-start | bytes 1572868
Sparse Core Ops, SparseCore 0:
  11.1 64.6 all-gather.6
  77.9 102.9 all-gather.4
  216.9 133.3 all-reduce.2
where the time goes:
time: 360 us; the launch traced here: 359 us
  waiting for transfers between devices  104 us (29%)
  blocking collectives  88.7 us (25%)
  other arithmetic  72.6 us (20%)
  local copies, waits for them, and re-layouts  47.6 us (13%)
  starting transfers between devices  21.9 us (6%)
  between operations  14.7 us (4%)
  matrix products  9.27 us (3%)
    psum x4, blocking collectives, one_axis_at_a_time(): value = lax.psum(value, axis)  88.7 us
    unnamed x2, other arithmetic  45.2 us
    unnamed x4, waiting for transfers between devices  38.4 us
    all_to_all x1, waiting for transfers between devices, on_device(): lax.all_to_all(outgoing[None], 'seq', split_axis=2, concat_axis=0, tiled=...  36.3 us
    all_gather x1, waiting for transfers between devices, on_device(): gathered = lax.all_gather(tile_tokens[0], 'seq', axis=0, tiled=True)  19.4 us
    unnamed x21, local copies, waits for them, and re-layouts  18.5 us
    all_to_all x1, starting transfers between devices, on_device(): lax.all_to_all(outgoing[None], 'seq', split_axis=2, concat_axis=0, tiled=...  15.2 us
    all_to_all x1, waiting for transfers between devices, copy_for_each(): return lax.all_to_all(copies, axis, split_axis=0, concat_axis=0, tiled=True)  9.99 us
  transfers between devices with their start and end apart: 5, of which 4 were waited for; matrix products, arithmetic and copies ran while one was open for 31% of the time, Pallas kernels for 0%

commit v1 on v0

--- a/solution.py
+++ b/solution.py
@@ -8,6 +8,22 @@
 DP = ("dp_0", "dp_1", "dp_2")
 DP_SEQ = ("dp_0", "dp_1", "dp_2", "seq")
 EPSILON = 1e-06
+
+
+def exchange_in_pairs(shard, axis, split, join):
+    ways, here = (lax.axis_size(axis), lax.axis_index(axis))
+    width = shard.shape[split] // ways
+    shape = list(shard.shape)
+    shape[split] = width
+    height = shape[join]
+    shape[join] = height * ways
+    full = jnp.zeros(shape, shard.dtype)
+    for mask in range(ways):
+        part = lax.dynamic_slice_in_dim(shard, (here ^ mask) * width, width, axis=split)
+        if mask:
+            part = lax.ppermute(part, axis, [(d, d ^ mask) for d in range(ways)])
+        full = lax.dynamic_update_slice_in_dim(full, part, (here ^ mask) * height, axis=join)
+    return full
 
 
 def copy_for_each(value, axis):
@@ -92,7 +108,7 @@
         jnp.arange(image_total, dtype=jnp.int32) - jnp.take(starts, owners)
     )
     outgoing = jnp.where(slot_live, jnp.take(own_cot, local_slots, axis=0), zero_half)
-    returned = lax.all_to_all(outgoing[None], "seq", split_axis=2, concat_axis=0, tiled=True)
+    returned = exchange_in_pairs(outgoing[None], "seq", 2, 0)
     image_cot = jnp.take(returned.reshape(-1, columns), flat_index, axis=0).astype(jnp.float32)
     emb_float = embedded.astype(jnp.float32)
     column_gain = lax.dynamic_slice_in_dim(norm_gain, seq_index * columns, columns)

time: 360 us -> 347 us (0.964)
  starting transfers between devices: 21.9 us -> 89.1 us
  other arithmetic: 72.6 us -> 27.4 us
  local copies, waits for them, and re-layouts: 47.6 us -> 19.8 us
  waiting for transfers between devices: 104 us -> 96 us
    ppermute x0 -> x15, starting transfers between devices: none -> 81.8 us  [exchange_in_pairs(): part = lax.ppermute(part, axis, [(d, d ^ mask) for d in range(ways)])]
    unnamed x2 -> x1, other arithmetic: 45.2 us -> 0.04 us
    all_to_all x1 -> x0, waiting for transfers between devices: 36.3 us -> none  [on_device(): lax.all_to_all(outgoing[None], 'seq', split_axis=2, concat_axis=0, tiled=...]
    all_gather x1, waiting for transfers between devices: 19.4 us -> 38.6 us  [on_device(): gathered = lax.all_gather(tile_tokens[0], 'seq', axis=0, tiled=True)]
    all_to_all x1 -> x0, starting transfers between devices: 15.2 us -> none  [on_device(): lax.all_to_all(outgoing[None], 'seq', split_axis=2, concat_axis=0, tiled=...]
    unnamed x21 -> x17, local copies, waits for them, and re-layouts: 18.5 us -> 5.94 us
    ppermute x0 -> x15, waiting for transfers between devices: none -> 9.14 us  [exchange_in_pairs(): part = lax.ppermute(part, axis, [(d, d ^ mask) for d in range(ways)])]
    all_to_all x3 -> x0, local copies, waits for them, and re-layouts: 8.62 us -> none  [on_device(): lax.all_to_all(outgoing[None], 'seq', split_axis=2, concat_axis=0, tiled=...]
  transfers between devices with their start and end apart: 5 -> 19, of which waited for: 4 -> 5; matrix products, arithmetic and copies ran while one was open for 31% -> 11% of each run, Pallas kernels for 0% -> 0%
where the time goes in v1:
time: 347 us; the launch traced here: 346 us
  waiting for transfers between devices  96 us (28%)
  starting transfers between devices  89.1 us (26%)
  blocking collectives  88.8 us (26%)
  other arithmetic  27.4 us (8%)
  local copies, waits for them, and re-layouts  19.8 us (6%)
  between operations  15.3 us (4%)
  matrix products  9.25 us (3%)
    psum x4, blocking collectives, one_axis_at_a_time(): value = lax.psum(value, axis)  88.8 us
    ppermute x15, starting transfers between devices, exchange_in_pairs(): part = lax.ppermute(part, axis, [(d, d ^ mask) for d in range(ways)])  81.8 us
    all_gather x1, waiting for transfers between devices, on_device(): gathered = lax.all_gather(tile_tokens[0], 'seq', axis=0, tiled=True)  38.6 us
    unnamed x4, waiting for transfers between devices  38.3 us
    all_to_all x1, waiting for transfers between devices, copy_for_each(): return lax.all_to_all(copies, axis, split_axis=0, concat_axis=0, tiled=True)  10 us
    ppermute x15, waiting for transfers between devices, exchange_in_pairs(): part = lax.ppermute(part, axis, [(d, d ^ mask) for d in range(ways)])  9.14 us
    all_to_all x1, starting transfers between devices, copy_for_each(): return lax.all_to_all(copies, axis, split_axis=0, concat_axis=0, tiled=True)  7.17 us
  transfers between devices with their start and end apart: 19, of which 5 were waited for; matrix products, arithmetic and copies ran while one was open for 11% of the time, Pallas kernels for 0%

profile of v1, /device:TPU:6, one launch (start us, length us, event | category | flops | bytes accessed | tf_op | source)
XLA Modules:
  0.0 345.6 jit_solution(13072340814138610611)
XLA Ops:
  7.2 0.7 all-gather.7.cloned.1.call-update
  8.0 0.7 all-gather.5.cloned.1.call-update
  8.7 0.7 add_select_fusion
  10.4 0.7 fusion.38
  11.8 1.5 gather_fusion
  13.3 0.7 fusion.35
  14.0 3.6 %gather_fusion.1 = bf16[48,8192]{1,0:T(8,128)(2,1)S(1)} fusion(bf16[128,8192]{1,0:T(8,128)(2,1)} %bitcast.109, s32[1024]{0:T(1024)S(1)} %pad_clamp_fusion.1), kind=kCustom, calls=%fused_computation.1 | custom fusion | bytes 1573056 | tf_op jit(solution)/shard_map/jit(_take)/gather | solution.py:110
  17.7 1.3 compare_and_fusion
  19.4 3.8 %collective-permute-start = (bf16[1,48,512]{2,1,0:T(8,128)(2,1)S(1)}, bf16[1,48,512]{2,1,0:T(8,128)(2,1)S(1)}, u32[]{:S(2)}, u32[]{:S(2)}) collective-permute-start(bf16[1,48,512]{2,1,0:T(8,128)(2,1)S(1)} %get-tuple-element.42), channel_id=1, source_target_pairs={{0,1},{1,0},{2,3},{3,2},{4,5},{5,4},{6,7},{7,6},{8,9},{9,8},{10,11... | collective-permute-start | bytes 147464 | tf_op jit(solution)/shard_map/ppermute | solution.py:24
  23.2 5.2 %collective-permute-start.1 = (bf16[1,48,512]{2,1,0:T(8,128)(2,1)S(1)}, bf16[1,48,512]{2,1,0:T(8,128)(2,1)S(1)}, u32[]{:S(2)}, u32[]{:S(2)}) collective-permute-start(bf16[1,48,512]{2,1,0:T(8,128)(2,1)S(1)} %get-tuple-element.41), channel_id=1, source_target_pairs={{0,2},{1,3},{2,0},{3,1},{4,6},{5,7},{6,4},{7,5},{8,10},{9,11},{10,... | collective-permute-start | bytes 147464 | tf_op jit(solution)/shard_map/ppermute | solution.py:24
  28.4 1.9 collective-permute-start.2
  30.3 9.1 %collective-permute-start.3 = (bf16[1,48,512]{2,1,0:T(8,128)(2,1)S(1)}, bf16[1,48,512]{2,1,0:T(8,128)(2,1)S(1)}, u32[]{:S(2)}, u32[]{:S(2)}) collective-permute-start(bf16[1,48,512]{2,1,0:T(8,128)(2,1)S(1)} %get-tuple-element.39), channel_id=1, source_target_pairs={{0,4},{1,5},{2,6},{3,7},{4,0},{5,1},{6,2},{7,3},{8,12},{9,13},{10,... | collective-permute-start | bytes 147464 | tf_op jit(solution)/shard_map/ppermute | solution.py:24
  39.4 1.9 collective-permute-start.4
  41.5 4.3 %compare_select_fusion.2 = (s32[512,1]{0,1:T(1,128)S(1)}, s32[512,1]{0,1:T(1,128)S(1)}, s32[512,1]{0,1:T(1,128)S(1)}, s32[512,1]{0,1:T(1,128)S(1)}) fusion(s32[]{:T(128)} %bitcast.12, s32[]{:T(128)} %bitcast.13, s32[]{:T(128)} %bitcast.14, s32[]{:T(128)} %bitcast.15, s32[]{:T(128)} %bitcast.16, s32[]{:T(128)} %bitcast.18, s32[]{:T(128)} %bitcast.17, ...), kind=kLoop, calls=%fused_computation.91 | loop fusion | flops 16384 | bytes 10268 | tf_op jit(solution)/shard_map/jit(_take)/gather | solution.py:108
  45.8 5.8 %compare_and_fusion.1 = (pred[512]{0:T(512)(128)(4,1)S(1)}, s32[512]{0:T(512)S(1)}) fusion(pred[512]{0:T(512)(128)(4,1)S(1)} %get-tuple-element.22, pred[512]{0:T(512)(128)(4,1)S(1)} %get-tuple-element.20, pred[512]{0:T(512)(128)(4,1)S(1)} %get-tuple-element.21, pred[512]{0:T(512)(128)(4,1)S(1)} %get-tuple-element.19, ...), kind=kLoop, calls=%fused_computation.131 | loop fusion | flops 20480 | bytes 11300 | tf_op jit(solution)/shard_map/jit(_take)/and | solution.py:112
  51.8 0.8 dynamic_slice.78
  52.5 10.2 %collective-permute-start.5 = (bf16[1,48,512]{2,1,0:T(8,128)(2,1)S(1)}, bf16[1,48,512]{2,1,0:T(8,128)(2,1)S(1)}, u32[]{:S(2)}, u32[]{:S(2)}) collective-permute-start(bf16[1,48,512]{2,1,0:T(8,128)(2,1)S(1)} %get-tuple-element.37), channel_id=1, source_target_pairs={{0,6},{1,7},{2,4},{3,5},{4,2},{5,3},{6,0},{7,1},{8,14},{9,15},{10,... | collective-permute-start | bytes 147464 | tf_op jit(solution)/shard_map/ppermute | solution.py:24
  62.7 1.9 collective-permute-start.6
  64.7 13.1 %collective-permute-start.7 = (bf16[1,48,512]{2,1,0:T(8,128)(2,1)S(1)}, bf16[1,48,512]{2,1,0:T(8,128)(2,1)S(1)}, u32[]{:S(2)}, u32[]{:S(2)}) collective-permute-start(bf16[1,48,512]{2,1,0:T(8,128)(2,1)S(1)} %get-tuple-element.35), channel_id=1, source_target_pairs={{0,8},{1,9},{2,10},{3,11},{4,12},{5,13},{6,14},{7,15},{8,0},{9,1},... | collective-permute-start | bytes 147464 | tf_op jit(solution)/shard_map/ppermute | solution.py:24
  77.8 1.9 collective-permute-start.8
  79.8 7.7 %collective-permute-start.9 = (bf16[1,48,512]{2,1,0:T(8,128)(2,1)S(1)}, bf16[1,48,512]{2,1,0:T(8,128)(2,1)S(1)}, u32[]{:S(2)}, u32[]{:S(2)}) collective-permute-start(bf16[1,48,512]{2,1,0:T(8,128)(2,1)S(1)} %get-tuple-element.33), channel_id=1, source_target_pairs={{0,10},{1,11},{2,8},{3,9},{4,14},{5,15},{6,12},{7,13},{8,2},{9,3},... | collective-permute-start | bytes 147464 | tf_op jit(solution)/shard_map/ppermute | solution.py:24
  87.5 4.2 %collective-permute-start.10 = (bf16[1,48,512]{2,1,0:T(8,128)(2,1)S(1)}, bf16[1,48,512]{2,1,0:T(8,128)(2,1)S(1)}, u32[]{:S(2)}, u32[]{:S(2)}) collective-permute-start(bf16[1,48,512]{2,1,0:T(8,128)(2,1)S(1)} %get-tuple-element.32), channel_id=1, source_target_pairs={{0,11},{1,10},{2,9},{3,8},{4,15},{5,14},{6,13},{7,12},{8,3},{9,2},... | collective-permute-start | bytes 147464 | tf_op jit(solution)/shard_map/ppermute | solution.py:24
  91.7 6.1 %collective-permute-start.11 = (bf16[1,48,512]{2,1,0:T(8,128)(2,1)S(1)}, bf16[1,48,512]{2,1,0:T(8,128)(2,1)S(1)}, u32[]{:S(2)}, u32[]{:S(2)}) collective-permute-start(bf16[1,48,512]{2,1,0:T(8,128)(2,1)S(1)} %get-tuple-element.31), channel_id=1, source_target_pairs={{0,12},{1,13},{2,14},{3,15},{4,8},{5,9},{6,10},{7,11},{8,4},{9,5},... | collective-permute-start | bytes 147464 | tf_op jit(solution)/shard_map/ppermute | solution.py:24
  97.8 4.6 %collective-permute-start.12 = (bf16[1,48,512]{2,1,0:T(8,128)(2,1)S(1)}, bf16[1,48,512]{2,1,0:T(8,128)(2,1)S(1)}, u32[]{:S(2)}, u32[]{:S(2)}) collective-permute-start(bf16[1,48,512]{2,1,0:T(8,128)(2,1)S(1)} %get-tuple-element.30), channel_id=1, source_target_pairs={{0,13},{1,12},{2,15},{3,14},{4,9},{5,8},{6,11},{7,10},{8,5},{9,4},... | collective-permute-start | bytes 147464 | tf_op jit(solution)/shard_map/ppermute | solution.py:24
  102.4 8.3 %collective-permute-start.13 = (bf16[1,48,512]{2,1,0:T(8,128)(2,1)S(1)}, bf16[1,48,512]{2,1,0:T(8,128)(2,1)S(1)}, u32[]{:S(2)}, u32[]{:S(2)}) collective-permute-start(bf16[1,48,512]{2,1,0:T(8,128)(2,1)S(1)} %get-tuple-element.29), channel_id=1, source_target_pairs={{0,14},{1,15},{2,12},{3,13},{4,10},{5,11},{6,8},{7,9},{8,6},{9,7},... | collective-permute-start | bytes 147464 | tf_op jit(solution)/shard_map/ppermute | solution.py:24
  110.8 1.9 collective-permute-start.14
  112.8 3.5 %collective-permute-done.13 = bf16[1,48,512]{2,1,0:T(8,128)(2,1)S(1)} collective-permute-done((bf16[1,48,512]{2,1,0:T(8,128)(2,1)S(1)}, bf16[1,48,512]{2,1,0:T(8,128)(2,1)S(1)}, u32[]{:S(2)}, u32[]{:S(2)}) %collective-permute-start.13) | collective-permute-done | bytes 49184 | tf_op jit(solution)/shard_map/ppermute | solution.py:24
  116.3 5.6 %collective-permute-done.14 = bf16[1,48,512]{2,1,0:T(8,128)(2,1)S(1)} collective-permute-done((bf16[1,48,512]{2,1,0:T(8,128)(2,1)S(1)}, bf16[1,48,512]{2,1,0:T(8,128)(2,1)S(1)}, u32[]{:S(2)}, u32[]{:S(2)}) %collective-permute-start.14) | collective-permute-done | bytes 49184 | tf_op jit(solution)/shard_map/ppermute | solution.py:24
  122.0 2.0 gather_fusion.2
  123.9 1.0 copy.24
  124.9 3.7 %reshape.425 = bf16[3200,512]{1,0:T(8,128)(2,1)S(1)} reshape(bf16[32,100,512]{2,1,0:T(8,128)(2,1)} %all-gather.7.cloned.1.call-done) | data formatting | bytes 6553600
  128.7 38.6 %all-gather.5.cloned.1.call-done = bf16[1,512,3200]{2,1,0:T(8,128)(2,1)} async-done(((bf16[1,32,3200]{2,1,0:T(8,128)(2,1)}), bf16[1,512,3200]{2,1,0:T(8,128)(2,1)}) %all-gather.5.cloned.1.call-update) | async-done | bytes 3276816 | tf_op jit(solution)/shard_map/all_gather | solution.py:87
  167.3 4.9 %fusion.23 = (f32[512]{0:T(512)S(1)}, f32[512]{0:T(512)S(1)}, bf16[512,512]{0,1:T(8,128)(2,1)}) fusion(f32[512]{0:T(512)S(1)} %dynamic_slice.78, bf16[512,512]{0,1:T(8,128)(2,1)} %copy.24, pred[512]{0:T(512)(128)(4,1)S(1)} %get-tuple-element.23, bf16[3200,512]{1,0:T(8,128)(2,1)S(1)} %reshape.425, bf16[1,512,3200]{2,1,0:T(8,128)(2,1)} %all-gather.5.cloned.1.call-done), kind=kOutput, calls=%fused_computation.35 | convolution fusion | flops 1680079872 | bytes 7608832 | tf_op jit(solution)/shard_map/dot_general | solution.py:89
  172.8 7.2 %all-to-all-start = ((f32[16,1,1024]{2,1,0:T(1,128)}), f32[16,1,1024]{2,1,0:T(1,128)S(1)}, u32[]{:S(2)}, u32[]{:S(2)}) async-start(f32[16,1,1024]{2,1,0:T(1,128)} %broadcast_in_dim.94), calls=%async_computation | async-start | bytes 131072 | tf_op jit(solution)/shard_map/all_to_all | solution.py:31
  180.1 2.6 scatter_custom_fusion
  182.8 10.0 %all-to-all-done = f32[16,1,1024]{2,1,0:T(1,128)S(1)} async-done(((f32[16,1,1024]{2,1,0:T(1,128)}), f32[16,1,1024]{2,1,0:T(1,128)S(1)}, u32[]{:S(2)}, u32[]{:S(2)}) %all-to-all-start) | async-done | bytes 65568 | tf_op jit(solution)/shard_map/all_to_all | solution.py:31
  192.9 4.4 %multiply_reduce_fusion = (f32[3200]{0:T(1024)S(1)}, f32[512,3200]{1,0:T(8,128)S(1)}) fusion(bf16[1,512,3200]{2,1,0:T(8,128)(2,1)} %all-gather.5.cloned.1.call-done, bf16[512,512]{0,1:T(8,128)(2,1)} %get-tuple-element.63, f32[512]{0:T(512)S(1)} %get-tuple-element.44, f32[512]{0:T(512)S(1)} %get-tuple-element.43, f32[512]{0:T(512)S(1)} %dynamic_slice.78, ...), kind=kOutput, calls=%fused_computation.12 | convolution fusion | flops 1683354496 | bytes 10898432 | tf_op jit(solution)/shard_map/dot_general | solution.py:137
  197.3 6.4 %fusion.6 = bf16[3200,512]{0,1:T(8,128)(2,1)} fusion(f32[512,3200]{1,0:T(8,128)S(1)} %get-tuple-element.65, f32[3200]{0:T(1024)S(1)} %convert_reduce_fusion.1, f32[512]{0:T(512)S(1)} %bitcast.117, f32[3200]{0:T(1024)S(1)} %reduce.13, f32[3200]{0:T(1024)S(1)} %add_sqrt_fusion), kind=kLoop, calls=%fused_computation.13 | loop fusion | flops 29491200 | bytes 9870848 | tf_op jit(solution)/shard_map/convert_element_type | solution.py:141
  203.9 1.3 dynamic-slice.65
  205.9 2.1 fusion.10
  208.0 2.5 fusion.9
  210.9 14.1 %psum.28 = f32[8192]{0:T(1024)S(1)} all-reduce(f32[8192]{0:T(1024)S(1)} %add_dynamic-update-slice_fusion), channel_id=1, replica_groups=mesh['dp_0'=4,'dp_1'=4,'dp_2'=2,'seq'=16] {'dp_0'}, use_global_device_ids=true, to_apply=%region_11.12 | all-reduce | flops 8192 | bytes 65536 | tf_op jit(solution)/shard_map/psum | solution.py:50
  225.0 17.4 %psum.29 = f32[8192]{0:T(1024)S(1)} all-reduce(f32[8192]{0:T(1024)S(1)} %psum.28), channel_id=1, replica_groups=mesh['dp_0'=4,'dp_1'=4,'dp_2'=2,'seq'=16] {'dp_1'}, use_global_device_ids=true, to_apply=%region_12.13 | all-reduce | flops 8192 | bytes 65536 | tf_op jit(solution)/shard_map/psum | solution.py:50
  242.5 3.4 psum.30
  245.9 53.8 %psum.31 = f32[8192]{0:T(1024)S(1)} all-reduce(f32[8192]{0:T(1024)S(1)} %psum.30), channel_id=1, replica_groups=mesh['dp_0'=4,'dp_1'=4,'dp_2'=2,'seq'=16] {'seq'}, use_global_device_ids=true, to_apply=%region_14.15 | all-reduce | flops 8192 | bytes 65536 | tf_op jit(solution)/shard_map/psum | solution.py:50
  300.3 36.9 %all-reduce.3.cloned.1.call-done = bf16[3200,512]{0,1:T(8,128)(2,1)} async-done(((bf16[3200,512]{0,1:T(8,128)(2,1)}), bf16[3200,512]{0,1:T(8,128)(2,1)}) %all-reduce.3.cloned.1.call-update) | async-done | bytes 3276816
  337.2 1.1 convert_multiply_fusion.7
  338.3 0.8 copy.26
  (76 shorter events, 4.5 us)
Async XLA Ops:
  7.2 34.3 %copy-start = (s32[1,512]{1,0:T(1,128)S(1)}, s32[1,512]{1,0:T(1,128)}, u32[]{:S(2)}) copy-start(s32[1,512]{1,0:T(1,128)} %param.14) | copy-start | bytes 6148
  7.2 117.8 %all-gather.7.cloned.1.call-start = ((), (), s32[]{:S(2)}) async-start(), calls=%async_computation.2 | async-start | bytes 3514368 | tf_op jit(solution)/shard_map/all_gather | solution.py:91
  7.9 159.4 %all-gather.5.cloned.1.call-start = ((), (), s32[]{:S(2)}) async-start(), calls=%async_computation.1 | async-start | bytes 3481600 | tf_op jit(solution)/shard_map/all_gather | solution.py:87
  19.4 33.2 %collective-permute-start = (bf16[1,48,512]{2,1,0:T(8,128)(2,1)S(1)}, bf16[1,48,512]{2,1,0:T(8,128)(2,1)S(1)}, u32[]{:S(2)}, u32[]{:S(2)}) collective-permute-start(bf16[1,48,512]{2,1,0:T(8,128)(2,1)S(1)} %get-tuple-element.42), channel_id=1, source_target_pairs={{0,1},{1,0},{2,3},{3,2},{4,5},{5,4},{6,7},{7,6},{8,9},{9,8},{10,11... | collective-permute-start | bytes 147464 | tf_op jit(solution)/shard_map/ppermute | solution.py:24
  23.2 39.5 %collective-permute-start.1 = (bf16[1,48,512]{2,1,0:T(8,128)(2,1)S(1)}, bf16[1,48,512]{2,1,0:T(8,128)(2,1)S(1)}, u32[]{:S(2)}, u32[]{:S(2)}) collective-permute-start(bf16[1,48,512]{2,1,0:T(8,128)(2,1)S(1)} %get-tuple-element.41), channel_id=1, source_target_pairs={{0,2},{1,3},{2,0},{3,1},{4,6},{5,7},{6,4},{7,5},{8,10},{9,11},{10,... | collective-permute-start | bytes 147464 | tf_op jit(solution)/shard_map/ppermute | solution.py:24
  28.4 36.3 %collective-permute-start.2 = (bf16[1,48,512]{2,1,0:T(8,128)(2,1)S(1)}, bf16[1,48,512]{2,1,0:T(8,128)(2,1)S(1)}, u32[]{:S(2)}, u32[]{:S(2)}) collective-permute-start(bf16[1,48,512]{2,1,0:T(8,128)(2,1)S(1)} %get-tuple-element.40), channel_id=1, source_target_pairs={{0,3},{1,2},{2,1},{3,0},{4,7},{5,6},{6,5},{7,4},{8,11},{9,10},{10,... | collective-permute-start | bytes 147464 | tf_op jit(solution)/shard_map/ppermute | solution.py:24
  30.3 47.5 %collective-permute-start.3 = (bf16[1,48,512]{2,1,0:T(8,128)(2,1)S(1)}, bf16[1,48,512]{2,1,0:T(8,128)(2,1)S(1)}, u32[]{:S(2)}, u32[]{:S(2)}) collective-permute-start(bf16[1,48,512]{2,1,0:T(8,128)(2,1)S(1)} %get-tuple-element.39), channel_id=1, source_target_pairs={{0,4},{1,5},{2,6},{3,7},{4,0},{5,1},{6,2},{7,3},{8,12},{9,13},{10,... | collective-permute-start | bytes 147464 | tf_op jit(solution)/shard_map/ppermute | solution.py:24
  39.4 40.4 %collective-permute-start.4 = (bf16[1,48,512]{2,1,0:T(8,128)(2,1)S(1)}, bf16[1,48,512]{2,1,0:T(8,128)(2,1)S(1)}, u32[]{:S(2)}, u32[]{:S(2)}) collective-permute-start(bf16[1,48,512]{2,1,0:T(8,128)(2,1)S(1)} %get-tuple-element.38), channel_id=1, source_target_pairs={{0,5},{1,4},{2,7},{3,6},{4,1},{5,0},{6,3},{7,2},{8,13},{9,12},{10,... | collective-permute-start | bytes 147464 | tf_op jit(solution)/shard_map/ppermute | solution.py:24
  52.5 35.0 %collective-permute-start.5 = (bf16[1,48,512]{2,1,0:T(8,128)(2,1)S(1)}, bf16[1,48,512]{2,1,0:T(8,128)(2,1)S(1)}, u32[]{:S(2)}, u32[]{:S(2)}) collective-permute-start(bf16[1,48,512]{2,1,0:T(8,128)(2,1)S(1)} %get-tuple-element.37), channel_id=1, source_target_pairs={{0,6},{1,7},{2,4},{3,5},{4,2},{5,3},{6,0},{7,1},{8,14},{9,15},{10,... | collective-permute-start | bytes 147464 | tf_op jit(solution)/shard_map/ppermute | solution.py:24
  62.7 29.0 %collective-permute-start.6 = (bf16[1,48,512]{2,1,0:T(8,128)(2,1)S(1)}, bf16[1,48,512]{2,1,0:T(8,128)(2,1)S(1)}, u32[]{:S(2)}, u32[]{:S(2)}) collective-permute-start(bf16[1,48,512]{2,1,0:T(8,128)(2,1)S(1)} %get-tuple-element.36), channel_id=1, source_target_pairs={{0,7},{1,6},{2,5},{3,4},{4,3},{5,2},{6,1},{7,0},{8,15},{9,14},{10,... | collective-permute-start | bytes 147464 | tf_op jit(solution)/shard_map/ppermute | solution.py:24
  64.7 33.1 %collective-permute-start.7 = (bf16[1,48,512]{2,1,0:T(8,128)(2,1)S(1)}, bf16[1,48,512]{2,1,0:T(8,128)(2,1)S(1)}, u32[]{:S(2)}, u32[]{:S(2)}) collective-permute-start(bf16[1,48,512]{2,1,0:T(8,128)(2,1)S(1)} %get-tuple-element.35), channel_id=1, source_target_pairs={{0,8},{1,9},{2,10},{3,11},{4,12},{5,13},{6,14},{7,15},{8,0},{9,1},... | collective-permute-start | bytes 147464 | tf_op jit(solution)/shard_map/ppermute | solution.py:24
  77.8 24.6 %collective-permute-start.8 = (bf16[1,48,512]{2,1,0:T(8,128)(2,1)S(1)}, bf16[1,48,512]{2,1,0:T(8,128)(2,1)S(1)}, u32[]{:S(2)}, u32[]{:S(2)}) collective-permute-start(bf16[1,48,512]{2,1,0:T(8,128)(2,1)S(1)} %get-tuple-element.34), channel_id=1, source_target_pairs={{0,9},{1,8},{2,11},{3,10},{4,13},{5,12},{6,15},{7,14},{8,1},{9,0},... | collective-permute-start | bytes 147464 | tf_op jit(solution)/shard_map/ppermute | solution.py:24
  79.8 31.0 %collective-permute-start.9 = (bf16[1,48,512]{2,1,0:T(8,128)(2,1)S(1)}, bf16[1,48,512]{2,1,0:T(8,128)(2,1)S(1)}, u32[]{:S(2)}, u32[]{:S(2)}) collective-permute-start(bf16[1,48,512]{2,1,0:T(8,128)(2,1)S(1)} %get-tuple-element.33), channel_id=1, source_target_pairs={{0,10},{1,11},{2,8},{3,9},{4,14},{5,15},{6,12},{7,13},{8,2},{9,3},... | collective-permute-start | bytes 147464 | tf_op jit(solution)/shard_map/ppermute | solution.py:24
  87.5 25.2 %collective-permute-start.10 = (bf16[1,48,512]{2,1,0:T(8,128)(2,1)S(1)}, bf16[1,48,512]{2,1,0:T(8,128)(2,1)S(1)}, u32[]{:S(2)}, u32[]{:S(2)}) collective-permute-start(bf16[1,48,512]{2,1,0:T(8,128)(2,1)S(1)} %get-tuple-element.32), channel_id=1, source_target_pairs={{0,11},{1,10},{2,9},{3,8},{4,15},{5,14},{6,13},{7,12},{8,3},{9,2},... | collective-permute-start | bytes 147464 | tf_op jit(solution)/shard_map/ppermute | solution.py:24
  91.7 21.1 %collective-permute-start.11 = (bf16[1,48,512]{2,1,0:T(8,128)(2,1)S(1)}, bf16[1,48,512]{2,1,0:T(8,128)(2,1)S(1)}, u32[]{:S(2)}, u32[]{:S(2)}) collective-permute-start(bf16[1,48,512]{2,1,0:T(8,128)(2,1)S(1)} %get-tuple-element.31), channel_id=1, source_target_pairs={{0,12},{1,13},{2,14},{3,15},{4,8},{5,9},{6,10},{7,11},{8,4},{9,5},... | collective-permute-start | bytes 147464 | tf_op jit(solution)/shard_map/ppermute | solution.py:24
  97.8 15.0 %collective-permute-start.12 = (bf16[1,48,512]{2,1,0:T(8,128)(2,1)S(1)}, bf16[1,48,512]{2,1,0:T(8,128)(2,1)S(1)}, u32[]{:S(2)}, u32[]{:S(2)}) collective-permute-start(bf16[1,48,512]{2,1,0:T(8,128)(2,1)S(1)} %get-tuple-element.30), channel_id=1, source_target_pairs={{0,13},{1,12},{2,15},{3,14},{4,9},{5,8},{6,11},{7,10},{8,5},{9,4},... | collective-permute-start | bytes 147464 | tf_op jit(solution)/shard_map/ppermute | solution.py:24
  102.4 13.9 %collective-permute-start.13 = (bf16[1,48,512]{2,1,0:T(8,128)(2,1)S(1)}, bf16[1,48,512]{2,1,0:T(8,128)(2,1)S(1)}, u32[]{:S(2)}, u32[]{:S(2)}) collective-permute-start(bf16[1,48,512]{2,1,0:T(8,128)(2,1)S(1)} %get-tuple-element.29), channel_id=1, source_target_pairs={{0,14},{1,15},{2,12},{3,13},{4,10},{5,11},{6,8},{7,9},{8,6},{9,7},... | collective-permute-start | bytes 147464 | tf_op jit(solution)/shard_map/ppermute | solution.py:24
  110.8 11.2 %collective-permute-start.14 = (bf16[1,48,512]{2,1,0:T(8,128)(2,1)S(1)}, bf16[1,48,512]{2,1,0:T(8,128)(2,1)S(1)}, u32[]{:S(2)}, u32[]{:S(2)}) collective-permute-start(bf16[1,48,512]{2,1,0:T(8,128)(2,1)S(1)} %get-tuple-element.28), channel_id=1, source_target_pairs={{0,15},{1,14},{2,13},{3,12},{4,11},{5,10},{6,9},{7,8},{8,7},{9,6},... | collective-permute-start | bytes 147464 | tf_op jit(solution)/shard_map/ppermute | solution.py:24
  128.7 51.4 %copy-start.5 = (f32[1,1,3200]{2,1,0:T(1,128)S(1)}, f32[1,1,3200]{2,1,0:T(1,128)}, u32[]{:S(2)}) copy-start(f32[1,1,3200]{2,1,0:T(1,128)} %param.16) | copy-start | bytes 38404
  128.7 54.1 %copy-start.4 = (s32[1,1,3200]{2,1,0:T(1,128)S(1)}, s32[1,1,3200]{2,1,0:T(1,128)}, u32[]{:S(2)}) copy-start(s32[1,1,3200]{2,1,0:T(1,128)} %param.15) | copy-start | bytes 38404
  172.2 25.2 %copy-start.6 = (f32[1,512]{1,0:T(1,128)S(1)}, f32[1,512]{1,0:T(1,128)}, u32[]{:S(2)}) copy-start(f32[1,512]{1,0:T(1,128)} %param.17) | copy-start | bytes 6148
  172.8 20.0 %all-to-all-start = ((f32[16,1,1024]{2,1,0:T(1,128)}), f32[16,1,1024]{2,1,0:T(1,128)S(1)}, u32[]{:S(2)}, u32[]{:S(2)}) async-start(f32[16,1,1024]{2,1,0:T(1,128)} %broadcast_in_dim.94), calls=%async_computation | async-start | bytes 131072 | tf_op jit(solution)/shard_map/all_to_all | solution.py:31
  180.0 157.2 %all-reduce.3.cloned.1.call-start = ((), (), s32[]{:S(2)}) async-start(), calls=%async_computation.3 | async-start | bytes 6553600
  197.3 10.6 %copy-start.1 = (bf16[1,128,8192]{2,1,0:T(8,128)(2,1)S(1)}, bf16[1,128,8192]{2,1,0:T(8,128)(2,1)}, u32[]{:S(2)}) copy-start(bf16[1,128,8192]{2,1,0:T(8,128)(2,1)} %param.12) | copy-start | bytes 6291460
  203.8 6.7 %copy-start.2 = (bf16[512,512]{0,1:T(8,128)(2,1)S(1)}, bf16[512,512]{0,1:T(8,128)(2,1)}, u32[]{:S(2)}) copy-start(bf16[512,512]{0,1:T(8,128)(2,1)} %copy.24) | copy-start | bytes 1572868
  203.8 6.7 %copy-start.3 = (bf16[512,512]{0,1:T(8,128)(2,1)S(1)}, bf16[512,512]{0,1:T(8,128)(2,1)}, u32[]{:S(2)}) copy-start(bf16[512,512]{0,1:T(8,128)(2,1)} %get-tuple-element.63) | copy-start | bytes 1572868
Sparse Core Ops, SparseCore 0:
  11.1 64.6 all-gather.6
  77.9 89.3 all-gather.4
  203.9 133.2 all-reduce.2
